TPU v7x, 256 devices: a whole 4x4x8 slice. The times are simulated.
256 devices in a mesh: ctx: 16 (over y_hi, x, core), smp: 16 (over y_lo, z).
Axes of the slice: x: 4, y: 4 (y_hi: 2, y_lo: 2; y = y_hi * 2 + y_lo), z: 8, core: 2. Of those that a mesh axis runs over, the one named last changes fastest.
Arguments:
- hidden_states: bfloat16 [64, 64, 5120], P('smp'), may hold values from -6 to 6
- query_weight: bfloat16 [5120, 5120], P('smp', 'ctx'), may hold values from -0.078125 to 0.078125
- kv_weight: bfloat16 [5120, 2048], P('smp', 'ctx'), may hold values from -0.078125 to 0.078125
- out_weight: bfloat16 [5120, 5120], P('smp', 'ctx'), may hold values from -0.078125 to 0.078125
- query_bias: bfloat16 [5120], P('ctx'), may hold values from -3 to 3
- kv_bias: bfloat16 [2048], P('ctx'), may hold values from -3 to 3
- prompt_kv: bfloat16 [4096, 2, 1024], P('ctx')
- parents: int32 [64, 64], P('smp'), may hold values from 0 to 62, as said below
- prefix_len: int32 [64], P('smp'), may hold values from 1024 to 4096, as said below
Outputs:
- layer_out: float32 [64, 64, 5120], P('smp', None, 'ctx')
Inputs may be any that keep to these rules, and one draw needn't show every extreme that they name: parents[s, 0] = 0, and for n >= 1 the parent of node n is an earlier node. `prefix_len`: some sample sees the whole prompt.
All inputs are finite; a program needn't handle non-finite values.
Results may differ from a plain program's by a relative error of at most 0.009.
The roundings to bfloat16 on the way count: a program that leaves them out, or rounds other values in their place, can miss the bound.
Values may be sent and summed in bfloat16 or wider, within the bound.
A program may use at most 64 MiB of HBM per device.

v0:
```python
import jax
import jax.numpy as jnp
from jax import lax
from jax.sharding import PartitionSpec as P

HQ = 40
KVH = 8
HD = 128
NODES = 64
SMP_DEV = 4
PROMPT_DEV = 256
rope_theta = 1000000.0
neg_big = -1e30


def passed_along(block, axis, distance):
    devices = range(lax.axis_size(axis))
    route = [((i - distance) % len(devices), i) for i in devices]
    return lax.ppermute(block, axis, route)


def ancestors(parents):
    node_count = parents.shape[-1]
    node_ids = jnp.arange(node_count, dtype=jnp.int32)
    step_up = (parents[..., :, None] == node_ids[None, None, :]).astype(jnp.float32)
    step_up = step_up * (node_ids[:, None] > 0).astype(jnp.float32)[None]
    reach = step_up + jnp.eye(node_count, dtype=jnp.float32)[None]
    for squaring in range(max(node_count - 1, 1).bit_length()):
        reach = jnp.minimum(
            jnp.einsum("snm,smk->snk", reach, reach, precision=lax.Precision.HIGHEST), 1.0
        )
    return reach


def rotate(values, positions):
    midpoint = values.shape[-1] // 2
    frequency = rope_theta ** (-jnp.arange(midpoint, dtype=jnp.float32) / midpoint)
    angles = positions[:, None] * frequency[None, :]
    cosine = jnp.cos(angles)[:, None, :]
    sine_part = jnp.sin(angles)[:, None, :]
    lower_half = values[..., :midpoint]
    upper_half = values[..., midpoint:]
    return jnp.concatenate(
        [
            lower_half * cosine - upper_half * sine_part,
            upper_half * cosine + lower_half * sine_part,
        ],
        axis=-1,
    )


def empty_state(row_count, heads_here, group):
    return (
        jnp.full((row_count, heads_here, group), neg_big, jnp.float32),
        jnp.zeros((row_count, heads_here, group), jnp.float32),
        jnp.zeros((row_count, heads_here, group, HD), jnp.float32),
    )


def attend_block(state, queries, keys, values, allowed):
    running_max, running_sum, running_acc = state
    scores = jnp.einsum(
        "rkgd,pkd->rkgp", queries, keys, preferred_element_type=jnp.float32
    ) * HD ** (-0.5)
    wide_mask = allowed[:, None, None, :]
    scores = jnp.where(wide_mask, scores, neg_big)
    new_max = jnp.maximum(running_max, jnp.max(scores, axis=-1))
    weights = jnp.where(wide_mask, jnp.exp(scores - new_max[..., None]), 0.0)
    factor = jnp.exp(running_max - new_max)
    new_sum = running_sum * factor + jnp.sum(weights, axis=-1)
    product = jnp.einsum(
        "rkgp,pkd->rkgd", weights.astype(jnp.bfloat16), values, preferred_element_type=jnp.float32
    )
    return (new_max, new_sum, running_acc * factor[..., None] + product)


def split_block(block):
    heads_here = block.shape[2] // HD
    return (
        block[:, 0].reshape(block.shape[0], heads_here, HD),
        block[:, 1].reshape(block.shape[0], heads_here, HD),
    )


def visible(row_limits, anchor):
    key_pos = anchor * PROMPT_DEV + jnp.arange(PROMPT_DEV, dtype=jnp.int32)
    return key_pos[None, :] < row_limits[:, None]


def shards(
    hidden_states,
    query_weight,
    kv_weight,
    out_weight,
    query_bias,
    kv_bias,
    prompt_kv,
    parents,
    prefix_len,
):
    group = HQ // KVH
    ctx_size = lax.axis_size("ctx")
    ctx_index = lax.axis_index("ctx")
    tree_rows = SMP_DEV * NODES
    own_rows = tree_rows // ctx_size
    row_start = ctx_index * own_rows
    flat = hidden_states.reshape(tree_rows, hidden_states.shape[2])
    columns = flat
    query_part = jnp.dot(
        columns,
        lax.all_gather(query_weight, "smp", axis=0, tiled=True),
        preferred_element_type=jnp.float32,
    )
    kv_part = jnp.dot(
        columns,
        lax.all_gather(kv_weight, "smp", axis=0, tiled=True),
        preferred_element_type=jnp.float32,
    )
    query_part = (query_part + query_bias[None, :].astype(jnp.float32)).astype(jnp.bfloat16)
    kv_part = (kv_part + kv_bias[None, :].astype(jnp.float32)).astype(jnp.bfloat16)
    query_lin = lax.all_to_all(query_part, "ctx", split_axis=0, concat_axis=1, tiled=True)
    tree_kv = lax.all_gather(kv_part, "ctx", axis=1, tiled=True)
    reach = ancestors(parents)
    positions = (prefix_len.astype(jnp.float32)[:, None] + jnp.sum(reach, axis=-1) - 1.0).reshape(
        tree_rows
    )
    tree_keys = rotate(
        tree_kv[:, : KVH * HD].astype(jnp.float32).reshape(tree_rows, KVH, HD), positions
    ).astype(jnp.bfloat16)
    tree_values = tree_kv[:, KVH * HD :].reshape(tree_rows, KVH, HD)
    own_positions = lax.dynamic_slice_in_dim(positions, row_start, own_rows)
    queries = rotate(query_lin.astype(jnp.float32).reshape(own_rows, HQ, HD), own_positions).astype(
        jnp.bfloat16
    )
    queries = queries.reshape(own_rows, KVH, group, HD)
    row_ids = row_start + jnp.arange(own_rows, dtype=jnp.int32)
    key_ids = jnp.arange(tree_rows, dtype=jnp.int32)
    reach_rows = lax.dynamic_slice_in_dim(reach.reshape(tree_rows, NODES), row_start, own_rows)
    same_sample = row_ids[:, None] // NODES == key_ids[None, :] // NODES
    tree_allowed = same_sample & (jnp.tile(reach_rows, (1, SMP_DEV)) > 0.5)
    every_limit = jnp.repeat(prefix_len, NODES)
    limits = lax.dynamic_slice_in_dim(every_limit, row_start, own_rows)
    tree_state = attend_block(
        empty_state(own_rows, KVH, group), queries, tree_keys, tree_values, tree_allowed
    )
    local_keys, local_values = split_block(prompt_kv)
    state = attend_block(tree_state, queries, local_keys, local_values, visible(limits, ctx_index))

    def turn(step, carry):
        block, running = carry
        block = passed_along(block, "ctx", 1)
        anchor = (ctx_index - step) % ctx_size
        block_keys, block_values = split_block(block)
        return (
            block,
            attend_block(running, queries, block_keys, block_values, visible(limits, anchor)),
        )

    state = lax.fori_loop(1, ctx_size, turn, (prompt_kv, state))[1]
    attn = (state[2] / state[1][..., None]).astype(jnp.bfloat16).reshape(own_rows, HQ * HD)
    every_row = lax.all_gather(attn, "ctx", axis=0, tiled=True)
    columns = every_row
    result = jnp.dot(
        columns,
        lax.all_gather(out_weight, "smp", axis=0, tiled=True),
        preferred_element_type=jnp.float32,
    )
    return result.reshape(SMP_DEV, NODES, out_weight.shape[1])


def solution(mesh):
    return jax.shard_map(
        shards,
        mesh=mesh,
        in_specs=(
            P("smp", None, None),
            P("smp", "ctx"),
            P("smp", "ctx"),
            P("smp", "ctx"),
            P("ctx"),
            P("ctx"),
            P("ctx", None, None),
            P("smp", None),
            P("smp"),
        ),
        out_specs=P("smp", None, "ctx"),
        check_vma=False,
    )
```

profile of v0, /device:TPU:1, one launch (start us, length us, event | category | flops | bytes accessed | tf_op | source)
XLA Modules:
  0.0 659.3 jit_solution(6417092861920433570)
XLA Ops:
  8.0 65.1 %all-gather.6.cloned.1.call-done = bf16[5120,128]{1,0:T(8,128)(2,1)} async-done(((bf16[320,128]{1,0:T(8,128)(2,1)}), bf16[5120,128]{1,0:T(8,128)(2,1)}) %all-gather.6.cloned.1.call-update) | async-done | bytes 1310736 | tf_op jit(solution)/shard_map/all_gather | solution.py:116
  87.1 47.1 %all-gather.8.cloned.1.call-done = bf16[256,2048]{1,0:T(8,128)(2,1)} async-done(((bf16[256,128]{1,0:T(8,128)(2,1)}), bf16[256,2048]{1,0:T(8,128)(2,1)}) %all-gather.8.cloned.1.call-update) | async-done | bytes 1048592 | tf_op jit(solution)/shard_map/all_gather | solution.py:122
  137.4 64.6 %all-gather.10.cloned.1.call-done = bf16[5120,320]{1,0:T(8,128)(2,1)} async-done(((bf16[320,320]{1,0:T(8,128)(2,1)}), bf16[5120,320]{1,0:T(8,128)(2,1)}) %all-gather.10.cloned.1.call-update) | async-done | bytes 3276816 | tf_op jit(solution)/shard_map/all_gather | solution.py:111
  202.0 3.7 fusion.17
  206.5 15.8 %all-to-all-start = ((bf16[16,16,320]{2,1,0:T(8,128)(2,1)}), bf16[16,16,320]{2,1,0:T(8,128)(2,1)}, u32[]{:S(2)}, u32[]{:S(2)}) async-start(bf16[16,16,320]{2,1,0:T(8,128)(2,1)} %bitcast.10), calls=%async_computation | async-start | bytes 393216 | tf_op jit(solution)/shard_map/all_to_all | solution.py:121
  226.4 8.1 %all-to-all-done = bf16[16,16,320]{2,1,0:T(8,128)(2,1)} async-done(((bf16[16,16,320]{2,1,0:T(8,128)(2,1)}), bf16[16,16,320]{2,1,0:T(8,128)(2,1)}, u32[]{:S(2)}, u32[]{:S(2)}) %all-to-all-start) | async-done | bytes 163872 | tf_op jit(solution)/shard_map/all_to_all | solution.py:121
  240.5 341.6 %while.21 = (s32[]{:T(128)}, bf16[256,2,1024]{0,2,1:T(8,128)(2,1)}, f32[16,8,5]{0,2,1:T(8,128)S(1)}, f32[16,8,5]{0,2,1:T(8,128)S(1)}, f32[16,8,5,128]{3,0,2,1:T(...) while((s32[]{:T(128)}, bf16[256,2,1024]{0,2,1:T(8,128)(2,1)}, ...), condition=%wide.region_8.9_spmd, body=%wide.region_5.8_spmd.sunk | while | flops 85530128 | bytes 12282222 | solution.py:159
  242.2 12.0 %collective-permute-done = bf16[256,2,1024]{0,2,1:T(8,128)(2,1)} collective-permute-done((bf16[256,2,1024]{0,2,1:T(8,128)(2,1)}, bf16[256,2,1024]{0,2,1:T(8,128)(2,1)}, u32[]{:S(2)}, u32[]{:S(2)}) %collective-permute-start) | collective-permute-done | bytes 1048608 | tf_op jit(solution)/shard_map/while/body/eval_jaxpr/ppermute | solution.py:19
  261.4 12.0 %collective-permute-done = bf16[256,2,1024]{0,2,1:T(8,128)(2,1)} collective-permute-done((bf16[256,2,1024]{0,2,1:T(8,128)(2,1)}, bf16[256,2,1024]{0,2,1:T(8,128)(2,1)}, u32[]{:S(2)}, u32[]{:S(2)}) %collective-permute-start) | collective-permute-done | bytes 1048608 | tf_op jit(solution)/shard_map/while/body/eval_jaxpr/ppermute | solution.py:19
  280.6 22.8 %collective-permute-done = bf16[256,2,1024]{0,2,1:T(8,128)(2,1)} collective-permute-done((bf16[256,2,1024]{0,2,1:T(8,128)(2,1)}, bf16[256,2,1024]{0,2,1:T(8,128)(2,1)}, u32[]{:S(2)}, u32[]{:S(2)}) %collective-permute-start) | collective-permute-done | bytes 1048608 | tf_op jit(solution)/shard_map/while/body/eval_jaxpr/ppermute | solution.py:19
  308.2 18.1 %collective-permute-done = bf16[256,2,1024]{0,2,1:T(8,128)(2,1)} collective-permute-done((bf16[256,2,1024]{0,2,1:T(8,128)(2,1)}, bf16[256,2,1024]{0,2,1:T(8,128)(2,1)}, u32[]{:S(2)}, u32[]{:S(2)}) %collective-permute-start) | collective-permute-done | bytes 1048608 | tf_op jit(solution)/shard_map/while/body/eval_jaxpr/ppermute | solution.py:19
  331.0 18.1 %collective-permute-done = bf16[256,2,1024]{0,2,1:T(8,128)(2,1)} collective-permute-done((bf16[256,2,1024]{0,2,1:T(8,128)(2,1)}, bf16[256,2,1024]{0,2,1:T(8,128)(2,1)}, u32[]{:S(2)}, u32[]{:S(2)}) %collective-permute-start) | collective-permute-done | bytes 1048608 | tf_op jit(solution)/shard_map/while/body/eval_jaxpr/ppermute | solution.py:19
  353.8 18.1 %collective-permute-done = bf16[256,2,1024]{0,2,1:T(8,128)(2,1)} collective-permute-done((bf16[256,2,1024]{0,2,1:T(8,128)(2,1)}, bf16[256,2,1024]{0,2,1:T(8,128)(2,1)}, u32[]{:S(2)}, u32[]{:S(2)}) %collective-permute-start) | collective-permute-done | bytes 1048608 | tf_op jit(solution)/shard_map/while/body/eval_jaxpr/ppermute | solution.py:19
  376.7 18.1 %collective-permute-done = bf16[256,2,1024]{0,2,1:T(8,128)(2,1)} collective-permute-done((bf16[256,2,1024]{0,2,1:T(8,128)(2,1)}, bf16[256,2,1024]{0,2,1:T(8,128)(2,1)}, u32[]{:S(2)}, u32[]{:S(2)}) %collective-permute-start) | collective-permute-done | bytes 1048608 | tf_op jit(solution)/shard_map/while/body/eval_jaxpr/ppermute | solution.py:19
  399.5 18.1 %collective-permute-done = bf16[256,2,1024]{0,2,1:T(8,128)(2,1)} collective-permute-done((bf16[256,2,1024]{0,2,1:T(8,128)(2,1)}, bf16[256,2,1024]{0,2,1:T(8,128)(2,1)}, u32[]{:S(2)}, u32[]{:S(2)}) %collective-permute-start) | collective-permute-done | bytes 1048608 | tf_op jit(solution)/shard_map/while/body/eval_jaxpr/ppermute | solution.py:19
  422.3 18.1 %collective-permute-done = bf16[256,2,1024]{0,2,1:T(8,128)(2,1)} collective-permute-done((bf16[256,2,1024]{0,2,1:T(8,128)(2,1)}, bf16[256,2,1024]{0,2,1:T(8,128)(2,1)}, u32[]{:S(2)}, u32[]{:S(2)}) %collective-permute-start) | collective-permute-done | bytes 1048608 | tf_op jit(solution)/shard_map/while/body/eval_jaxpr/ppermute | solution.py:19
  445.2 18.1 %collective-permute-done = bf16[256,2,1024]{0,2,1:T(8,128)(2,1)} collective-permute-done((bf16[256,2,1024]{0,2,1:T(8,128)(2,1)}, bf16[256,2,1024]{0,2,1:T(8,128)(2,1)}, u32[]{:S(2)}, u32[]{:S(2)}) %collective-permute-start) | collective-permute-done | bytes 1048608 | tf_op jit(solution)/shard_map/while/body/eval_jaxpr/ppermute | solution.py:19
  468.0 18.1 %collective-permute-done = bf16[256,2,1024]{0,2,1:T(8,128)(2,1)} collective-permute-done((bf16[256,2,1024]{0,2,1:T(8,128)(2,1)}, bf16[256,2,1024]{0,2,1:T(8,128)(2,1)}, u32[]{:S(2)}, u32[]{:S(2)}) %collective-permute-start) | collective-permute-done | bytes 1048608 | tf_op jit(solution)/shard_map/while/body/eval_jaxpr/ppermute | solution.py:19
  490.9 18.1 %collective-permute-done = bf16[256,2,1024]{0,2,1:T(8,128)(2,1)} collective-permute-done((bf16[256,2,1024]{0,2,1:T(8,128)(2,1)}, bf16[256,2,1024]{0,2,1:T(8,128)(2,1)}, u32[]{:S(2)}, u32[]{:S(2)}) %collective-permute-start) | collective-permute-done | bytes 1048608 | tf_op jit(solution)/shard_map/while/body/eval_jaxpr/ppermute | solution.py:19
  513.7 18.1 %collective-permute-done = bf16[256,2,1024]{0,2,1:T(8,128)(2,1)} collective-permute-done((bf16[256,2,1024]{0,2,1:T(8,128)(2,1)}, bf16[256,2,1024]{0,2,1:T(8,128)(2,1)}, u32[]{:S(2)}, u32[]{:S(2)}) %collective-permute-start) | collective-permute-done | bytes 1048608 | tf_op jit(solution)/shard_map/while/body/eval_jaxpr/ppermute | solution.py:19
  536.5 18.1 %collective-permute-done = bf16[256,2,1024]{0,2,1:T(8,128)(2,1)} collective-permute-done((bf16[256,2,1024]{0,2,1:T(8,128)(2,1)}, bf16[256,2,1024]{0,2,1:T(8,128)(2,1)}, u32[]{:S(2)}, u32[]{:S(2)}) %collective-permute-start) | collective-permute-done | bytes 1048608 | tf_op jit(solution)/shard_map/while/body/eval_jaxpr/ppermute | solution.py:19
  559.4 18.1 %collective-permute-done = bf16[256,2,1024]{0,2,1:T(8,128)(2,1)} collective-permute-done((bf16[256,2,1024]{0,2,1:T(8,128)(2,1)}, bf16[256,2,1024]{0,2,1:T(8,128)(2,1)}, u32[]{:S(2)}, u32[]{:S(2)}) %collective-permute-start) | collective-permute-done | bytes 1048608 | tf_op jit(solution)/shard_map/while/body/eval_jaxpr/ppermute | solution.py:19
  583.3 64.3 %all-gather.12.cloned.1.call-done = bf16[256,5120]{1,0:T(8,128)(2,1)} async-done(((bf16[16,5120]{1,0:T(8,128)(2,1)}), bf16[256,5120]{1,0:T(8,128)(2,1)}) %all-gather.12.cloned.1.call-update) | async-done | bytes 2621456 | tf_op jit(solution)/shard_map/all_gather | solution.py:161
  647.6 5.2 fusion.53
  (248 shorter events, 107.7 us)
Async XLA Ops:
  6.5 66.6 %copy-start = (bf16[4,64,5120]{2,1,0:T(8,128)(2,1)S(1)}, bf16[4,64,5120]{2,1,0:T(8,128)(2,1)}, u32[]{:S(2)}) copy-start(bf16[4,64,5120]{2,1,0:T(8,128)(2,1)} %param.11) | copy-start | bytes 7864324
  6.5 70.8 %copy-start.8 = (s32[4,64]{1,0:T(4,128)S(1)}, s32[4,64]{1,0:T(4,128)}, u32[]{:S(2)}) copy-start(s32[4,64]{1,0:T(4,128)} %param.18) | copy-start | bytes 3076
  6.5 66.6 %all-gather.6.cloned.1.call-start = ((), (), s32[]{:S(2)}) async-start(), calls=%async_computation.1 | async-start | bytes 1392640 | tf_op jit(solution)/shard_map/all_gather | solution.py:116
  7.3 126.9 %all-gather.8.cloned.1.call-start = ((), (), s32[]{:S(2)}) async-start(), calls=%async_computation.2 | async-start | bytes 1114112 | tf_op jit(solution)/shard_map/all_gather | solution.py:122
  76.0 126.0 %all-gather.10.cloned.1.call-start = ((), (), s32[]{:S(2)}) async-start(), calls=%async_computation.3 | async-start | bytes 4177920 | tf_op jit(solution)/shard_map/all_gather | solution.py:111
  76.7 506.6 %all-gather.14.cloned.1.call-start = ((), (), s32[]{:S(2)}) async-start(), calls=%async_computation.5 | async-start | bytes 4177920 | tf_op jit(solution)/shard_map/all_gather | solution.py:165
  206.5 28.0 %all-to-all-start = ((bf16[16,16,320]{2,1,0:T(8,128)(2,1)}), bf16[16,16,320]{2,1,0:T(8,128)(2,1)}, u32[]{:S(2)}, u32[]{:S(2)}) async-start(bf16[16,16,320]{2,1,0:T(8,128)(2,1)} %bitcast.10), calls=%async_computation | async-start | bytes 393216 | tf_op jit(solution)/shard_map/all_to_all | solution.py:121
  222.3 425.3 %all-gather.12.cloned.1.call-start = ((), (), s32[]{:S(2)}) async-start(), calls=%async_computation.4 | async-start | bytes 2785280 | tf_op jit(solution)/shard_map/all_gather | solution.py:161
  226.4 11.5 %copy-start.2 = (bf16[256,1,1024]{0,2,1:T(8,128)(2,1)S(1)}, bf16[256,1,1024]{0,2,1:T(8,128)(2,1)}, u32[]{:S(2)}) copy-start(bf16[256,1,1024]{0,2,1:T(8,128)(2,1)} %get-tuple-element.250) | copy-start | bytes 1572868
  240.5 13.6 %collective-permute-start = (bf16[256,2,1024]{0,2,1:T(8,128)(2,1)}, bf16[256,2,1024]{0,2,1:T(8,128)(2,1)}, u32[]{:S(2)}, u32[]{:S(2)}) collective-permute-start(bf16[256,2,1024]{0,2,1:T(8,128)(2,1)} %get-tuple-element.347), channel_id=1, source_target_pairs={{240,0},{0,16},{16,32},{32,48},{48,64},{64,80},{80,96},{96,112},{1... | collective-permute-start | bytes 3145736 | tf_op jit(solution)/shard_map/while/body/eval_jaxpr/ppermute | solution.py:19
  258.8 14.5 %collective-permute-start = (bf16[256,2,1024]{0,2,1:T(8,128)(2,1)}, bf16[256,2,1024]{0,2,1:T(8,128)(2,1)}, u32[]{:S(2)}, u32[]{:S(2)}) collective-permute-start(bf16[256,2,1024]{0,2,1:T(8,128)(2,1)} %get-tuple-element.347), channel_id=1, source_target_pairs={{240,0},{0,16},{16,32},{32,48},{48,64},{64,80},{80,96},{96,112},{1... | collective-permute-start | bytes 3145736 | tf_op jit(solution)/shard_map/while/body/eval_jaxpr/ppermute | solution.py:19
  278.1 25.3 %collective-permute-start = (bf16[256,2,1024]{0,2,1:T(8,128)(2,1)}, bf16[256,2,1024]{0,2,1:T(8,128)(2,1)}, u32[]{:S(2)}, u32[]{:S(2)}) collective-permute-start(bf16[256,2,1024]{0,2,1:T(8,128)(2,1)} %get-tuple-element.347), channel_id=1, source_target_pairs={{240,0},{0,16},{16,32},{32,48},{48,64},{64,80},{80,96},{96,112},{1... | collective-permute-start | bytes 3145736 | tf_op jit(solution)/shard_map/while/body/eval_jaxpr/ppermute | solution.py:19
  308.1 18.2 %collective-permute-start = (bf16[256,2,1024]{0,2,1:T(8,128)(2,1)}, bf16[256,2,1024]{0,2,1:T(8,128)(2,1)}, u32[]{:S(2)}, u32[]{:S(2)}) collective-permute-start(bf16[256,2,1024]{0,2,1:T(8,128)(2,1)} %get-tuple-element.347), channel_id=1, source_target_pairs={{240,0},{0,16},{16,32},{32,48},{48,64},{64,80},{80,96},{96,112},{1... | collective-permute-start | bytes 3145736 | tf_op jit(solution)/shard_map/while/body/eval_jaxpr/ppermute | solution.py:19
  330.9 18.2 %collective-permute-start = (bf16[256,2,1024]{0,2,1:T(8,128)(2,1)}, bf16[256,2,1024]{0,2,1:T(8,128)(2,1)}, u32[]{:S(2)}, u32[]{:S(2)}) collective-permute-start(bf16[256,2,1024]{0,2,1:T(8,128)(2,1)} %get-tuple-element.347), channel_id=1, source_target_pairs={{240,0},{0,16},{16,32},{32,48},{48,64},{64,80},{80,96},{96,112},{1... | collective-permute-start | bytes 3145736 | tf_op jit(solution)/shard_map/while/body/eval_jaxpr/ppermute | solution.py:19
  353.7 18.2 %collective-permute-start = (bf16[256,2,1024]{0,2,1:T(8,128)(2,1)}, bf16[256,2,1024]{0,2,1:T(8,128)(2,1)}, u32[]{:S(2)}, u32[]{:S(2)}) collective-permute-start(bf16[256,2,1024]{0,2,1:T(8,128)(2,1)} %get-tuple-element.347), channel_id=1, source_target_pairs={{240,0},{0,16},{16,32},{32,48},{48,64},{64,80},{80,96},{96,112},{1... | collective-permute-start | bytes 3145736 | tf_op jit(solution)/shard_map/while/body/eval_jaxpr/ppermute | solution.py:19
  376.6 18.2 %collective-permute-start = (bf16[256,2,1024]{0,2,1:T(8,128)(2,1)}, bf16[256,2,1024]{0,2,1:T(8,128)(2,1)}, u32[]{:S(2)}, u32[]{:S(2)}) collective-permute-start(bf16[256,2,1024]{0,2,1:T(8,128)(2,1)} %get-tuple-element.347), channel_id=1, source_target_pairs={{240,0},{0,16},{16,32},{32,48},{48,64},{64,80},{80,96},{96,112},{1... | collective-permute-start | bytes 3145736 | tf_op jit(solution)/shard_map/while/body/eval_jaxpr/ppermute | solution.py:19
  399.4 18.2 %collective-permute-start = (bf16[256,2,1024]{0,2,1:T(8,128)(2,1)}, bf16[256,2,1024]{0,2,1:T(8,128)(2,1)}, u32[]{:S(2)}, u32[]{:S(2)}) collective-permute-start(bf16[256,2,1024]{0,2,1:T(8,128)(2,1)} %get-tuple-element.347), channel_id=1, source_target_pairs={{240,0},{0,16},{16,32},{32,48},{48,64},{64,80},{80,96},{96,112},{1... | collective-permute-start | bytes 3145736 | tf_op jit(solution)/shard_map/while/body/eval_jaxpr/ppermute | solution.py:19
  422.3 18.2 %collective-permute-start = (bf16[256,2,1024]{0,2,1:T(8,128)(2,1)}, bf16[256,2,1024]{0,2,1:T(8,128)(2,1)}, u32[]{:S(2)}, u32[]{:S(2)}) collective-permute-start(bf16[256,2,1024]{0,2,1:T(8,128)(2,1)} %get-tuple-element.347), channel_id=1, source_target_pairs={{240,0},{0,16},{16,32},{32,48},{48,64},{64,80},{80,96},{96,112},{1... | collective-permute-start | bytes 3145736 | tf_op jit(solution)/shard_map/while/body/eval_jaxpr/ppermute | solution.py:19
  445.1 18.2 %collective-permute-start = (bf16[256,2,1024]{0,2,1:T(8,128)(2,1)}, bf16[256,2,1024]{0,2,1:T(8,128)(2,1)}, u32[]{:S(2)}, u32[]{:S(2)}) collective-permute-start(bf16[256,2,1024]{0,2,1:T(8,128)(2,1)} %get-tuple-element.347), channel_id=1, source_target_pairs={{240,0},{0,16},{16,32},{32,48},{48,64},{64,80},{80,96},{96,112},{1... | collective-permute-start | bytes 3145736 | tf_op jit(solution)/shard_map/while/body/eval_jaxpr/ppermute | solution.py:19
  467.9 18.2 %collective-permute-start = (bf16[256,2,1024]{0,2,1:T(8,128)(2,1)}, bf16[256,2,1024]{0,2,1:T(8,128)(2,1)}, u32[]{:S(2)}, u32[]{:S(2)}) collective-permute-start(bf16[256,2,1024]{0,2,1:T(8,128)(2,1)} %get-tuple-element.347), channel_id=1, source_target_pairs={{240,0},{0,16},{16,32},{32,48},{48,64},{64,80},{80,96},{96,112},{1... | collective-permute-start | bytes 3145736 | tf_op jit(solution)/shard_map/while/body/eval_jaxpr/ppermute | solution.py:19
  490.8 18.2 %collective-permute-start = (bf16[256,2,1024]{0,2,1:T(8,128)(2,1)}, bf16[256,2,1024]{0,2,1:T(8,128)(2,1)}, u32[]{:S(2)}, u32[]{:S(2)}) collective-permute-start(bf16[256,2,1024]{0,2,1:T(8,128)(2,1)} %get-tuple-element.347), channel_id=1, source_target_pairs={{240,0},{0,16},{16,32},{32,48},{48,64},{64,80},{80,96},{96,112},{1... | collective-permute-start | bytes 3145736 | tf_op jit(solution)/shard_map/while/body/eval_jaxpr/ppermute | solution.py:19
  513.6 18.2 %collective-permute-start = (bf16[256,2,1024]{0,2,1:T(8,128)(2,1)}, bf16[256,2,1024]{0,2,1:T(8,128)(2,1)}, u32[]{:S(2)}, u32[]{:S(2)}) collective-permute-start(bf16[256,2,1024]{0,2,1:T(8,128)(2,1)} %get-tuple-element.347), channel_id=1, source_target_pairs={{240,0},{0,16},{16,32},{32,48},{48,64},{64,80},{80,96},{96,112},{1... | collective-permute-start | bytes 3145736 | tf_op jit(solution)/shard_map/while/body/eval_jaxpr/ppermute | solution.py:19
  536.4 18.2 %collective-permute-start = (bf16[256,2,1024]{0,2,1:T(8,128)(2,1)}, bf16[256,2,1024]{0,2,1:T(8,128)(2,1)}, u32[]{:S(2)}, u32[]{:S(2)}) collective-permute-start(bf16[256,2,1024]{0,2,1:T(8,128)(2,1)} %get-tuple-element.347), channel_id=1, source_target_pairs={{240,0},{0,16},{16,32},{32,48},{48,64},{64,80},{80,96},{96,112},{1... | collective-permute-start | bytes 3145736 | tf_op jit(solution)/shard_map/while/body/eval_jaxpr/ppermute | solution.py:19
  559.3 18.2 %collective-permute-start = (bf16[256,2,1024]{0,2,1:T(8,128)(2,1)}, bf16[256,2,1024]{0,2,1:T(8,128)(2,1)}, u32[]{:S(2)}, u32[]{:S(2)}) collective-permute-start(bf16[256,2,1024]{0,2,1:T(8,128)(2,1)} %get-tuple-element.347), channel_id=1, source_target_pairs={{240,0},{0,16},{16,32},{32,48},{48,64},{64,80},{80,96},{96,112},{1... | collective-permute-start | bytes 3145736 | tf_op jit(solution)/shard_map/while/body/eval_jaxpr/ppermute | solution.py:19
  (6 other events, 19.2 us)
Sparse Core Ops, SparseCore 0:
  9.1 63.9 all-gather.5
  76.1 58.0 all-gather.7
  136.0 65.9 all-gather.9
  203.6 85.2 all-gather.13
  583.4 64.1 all-gather.11
where the time goes:
time: 661 us; the launch traced here: 659 us
  waiting for transfers between devices  515 us (78%)
  local copies, waits for them, and re-layouts  67.6 us (10%)
  matrix products  25.5 us (4%)
  starting transfers between devices  22.7 us (3%)
  other arithmetic  14.6 us (2%)
  between operations  13.5 us (2%)
    ppermute x15, waiting for transfers between devices, passed_along(): return lax.ppermute(block, axis, route)  264 us
    all_gather x1, waiting for transfers between devices, shards(): lax.all_gather(kv_weight, 'smp', axis=0, tiled=True)  65.1 us
    all_gather x1, waiting for transfers between devices, shards(): lax.all_gather(query_weight, 'smp', axis=0, tiled=True)  64.6 us
    all_gather x1, waiting for transfers between devices, shards(): every_row = lax.all_gather(attn, 'ctx', axis=0, tiled=True)  64.3 us
    all_gather x1, waiting for transfers between devices, shards(): tree_kv = lax.all_gather(kv_part, 'ctx', axis=1, tiled=True)  47.1 us
    while x30, local copies, waits for them, and re-layouts  35.1 us
    slice x16, local copies, waits for them, and re-layouts, split_block(): block[:, 1].reshape(block.shape[0], heads_here, HD)  21.3 us
    all_to_all x1, starting transfers between devices, shards(): lax.all_to_all(query_part, 'ctx', split_axis=0, concat_axis=1, tiled=True)  15.8 us
  transfers between devices with their start and end apart: 21, of which 20 were waited for; matrix products, arithmetic and copies ran while one was open for 15% of the time, Pallas kernels for 0%

commit v1 on v0

--- a/solution.py
+++ b/solution.py
@@ -118,7 +118,10 @@
     )
     query_part = (query_part + query_bias[None, :].astype(jnp.float32)).astype(jnp.bfloat16)
     kv_part = (kv_part + kv_bias[None, :].astype(jnp.float32)).astype(jnp.bfloat16)
-    query_lin = lax.all_to_all(query_part, "ctx", split_axis=0, concat_axis=1, tiled=True)
+    query_lin = jnp.concatenate(
+        lax.all_to_all(jnp.stack(jnp.split(query_part, lax.axis_size("ctx"), axis=0)), "ctx", 0, 0),
+        axis=1,
+    )
     tree_kv = lax.all_gather(kv_part, "ctx", axis=1, tiled=True)
     reach = ancestors(parents)
     positions = (prefix_len.astype(jnp.float32)[:, None] + jnp.sum(reach, axis=-1) - 1.0).reshape(

time: 661 us -> 685 us (1.036)
  local copies, waits for them, and re-layouts: 67.6 us -> 106 us
  waiting for transfers between devices: 515 us -> 496 us
    another operation x2 -> x20, local copies, waits for them, and re-layouts: 0.05 us -> 22.5 us  [the longest x18 22.5 us: shards(): jnp.stack(jnp.split(query_part, lax.axis_size('ctx'), axis=0))]
    ppermute x15, waiting for transfers between devices: 264 us -> 247 us  [passed_along(): return lax.ppermute(block, axis, route)]
    unnamed x20 -> x45, local copies, waits for them, and re-layouts: 1.62 us -> 17.7 us
  transfers between devices with their start and end apart: 21 -> 21, of which waited for: 20 -> 20; matrix products, arithmetic and copies ran while one was open for 15% -> 20% of each run, Pallas kernels for 0% -> 0%
where the time goes in v1:
time: 685 us; the launch traced here: 683 us
  waiting for transfers between devices  496 us (72%)
  local copies, waits for them, and re-layouts  106 us (15%)
  starting transfers between devices  26 us (4%)
  matrix products  25.5 us (4%)
  other arithmetic  15.1 us (2%)
  between operations  13.5 us (2%)
    ppermute x15, waiting for transfers between devices, passed_along(): return lax.ppermute(block, axis, route)  247 us
    all_gather x1, waiting for transfers between devices, shards(): lax.all_gather(kv_weight, 'smp', axis=0, tiled=True)  65.1 us
    all_gather x1, waiting for transfers between devices, shards(): lax.all_gather(query_weight, 'smp', axis=0, tiled=True)  64.6 us
    all_gather x1, waiting for transfers between devices, shards(): every_row = lax.all_gather(attn, 'ctx', axis=0, tiled=True)  63.2 us
    all_gather x1, waiting for transfers between devices, shards(): tree_kv = lax.all_gather(kv_part, 'ctx', axis=1, tiled=True)  46.5 us
    while x30, local copies, waits for them, and re-layouts  35.5 us
    another operation x18, local copies, waits for them, and re-layouts, shards(): jnp.stack(jnp.split(query_part, lax.axis_size('ctx'), axis=0))  22.5 us
    slice x16, local copies, waits for them, and re-layouts, split_block(): block[:, 1].reshape(block.shape[0], heads_here, HD)  21.3 us
  transfers between devices with their start and end apart: 21, of which 20 were waited for; matrix products, arithmetic and copies ran while one was open for 20% of the time, Pallas kernels for 0%

profile of v1, /device:TPU:1, one launch (start us, length us, event | category | flops | bytes accessed | tf_op | source)
XLA Modules:
  0.0 682.6 jit_solution(5611097748885854461)
XLA Ops:
  8.0 65.1 %all-gather.6.cloned.1.call-done = bf16[5120,128]{1,0:T(8,128)(2,1)} async-done(((bf16[320,128]{1,0:T(8,128)(2,1)}), bf16[5120,128]{1,0:T(8,128)(2,1)}) %all-gather.6.cloned.1.call-update) | async-done | bytes 1310736 | tf_op jit(solution)/shard_map/all_gather | solution.py:116
  87.7 46.5 %all-gather.8.cloned.1.call-done = bf16[256,2048]{1,0:T(8,128)(2,1)} async-done(((bf16[256,128]{1,0:T(8,128)(2,1)}), bf16[256,2048]{1,0:T(8,128)(2,1)}) %all-gather.8.cloned.1.call-update) | async-done | bytes 1048592 | tf_op jit(solution)/shard_map/all_gather | solution.py:125
  137.4 64.6 %all-gather.10.cloned.1.call-done = bf16[5120,320]{1,0:T(8,128)(2,1)} async-done(((bf16[320,320]{1,0:T(8,128)(2,1)}), bf16[5120,320]{1,0:T(8,128)(2,1)}) %all-gather.10.cloned.1.call-update) | async-done | bytes 3276816 | tf_op jit(solution)/shard_map/all_gather | solution.py:111
  202.0 3.7 fusion.17
  244.2 15.9 %all-to-all-start = ((bf16[16,16,320]{2,1,0:T(8,128)(2,1)}), bf16[16,16,320]{2,1,0:T(8,128)(2,1)}, u32[]{:S(2)}, u32[]{:S(2)}) async-start(bf16[16,16,320]{2,1,0:T(8,128)(2,1)} %constant_dynamic-update-slice_fusion), calls=%async_computation | async-start | bytes 393216 | tf_op jit(solution)/shard_map/all_to_all | solution.py:122
  264.2 7.6 %all-to-all-done = bf16[16,16,320]{2,1,0:T(8,128)(2,1)} async-done(((bf16[16,16,320]{2,1,0:T(8,128)(2,1)}), bf16[16,16,320]{2,1,0:T(8,128)(2,1)}, u32[]{:S(2)}, u32[]{:S(2)}) %all-to-all-start) | async-done | bytes 163872 | tf_op jit(solution)/shard_map/all_to_all | solution.py:122
  277.8 328.7 %while.21 = (s32[]{:T(128)}, bf16[256,2,1024]{0,2,1:T(8,128)(2,1)}, f32[16,8,5]{0,2,1:T(8,128)S(1)}, f32[16,8,5]{0,2,1:T(8,128)S(1)}, f32[16,8,5,128]{3,0,2,1:T(...) while((s32[]{:T(128)}, bf16[256,2,1024]{0,2,1:T(8,128)(2,1)}, ...), condition=%wide.region_8.9_spmd, body=%wide.region_5.8_spmd.sunk | while | flops 85530128 | bytes 12282222 | solution.py:162
  279.2 12.0 %collective-permute-done = bf16[256,2,1024]{0,2,1:T(8,128)(2,1)} collective-permute-done((bf16[256,2,1024]{0,2,1:T(8,128)(2,1)}, bf16[256,2,1024]{0,2,1:T(8,128)(2,1)}, u32[]{:S(2)}, u32[]{:S(2)}) %collective-permute-start) | collective-permute-done | bytes 1048608 | tf_op jit(solution)/shard_map/while/body/eval_jaxpr/ppermute | solution.py:19
  298.4 12.0 %collective-permute-done = bf16[256,2,1024]{0,2,1:T(8,128)(2,1)} collective-permute-done((bf16[256,2,1024]{0,2,1:T(8,128)(2,1)}, bf16[256,2,1024]{0,2,1:T(8,128)(2,1)}, u32[]{:S(2)}, u32[]{:S(2)}) %collective-permute-start) | collective-permute-done | bytes 1048608 | tf_op jit(solution)/shard_map/while/body/eval_jaxpr/ppermute | solution.py:19
  317.7 12.0 %collective-permute-done = bf16[256,2,1024]{0,2,1:T(8,128)(2,1)} collective-permute-done((bf16[256,2,1024]{0,2,1:T(8,128)(2,1)}, bf16[256,2,1024]{0,2,1:T(8,128)(2,1)}, u32[]{:S(2)}, u32[]{:S(2)}) %collective-permute-start) | collective-permute-done | bytes 1048608 | tf_op jit(solution)/shard_map/while/body/eval_jaxpr/ppermute | solution.py:19
  336.9 13.3 %collective-permute-done = bf16[256,2,1024]{0,2,1:T(8,128)(2,1)} collective-permute-done((bf16[256,2,1024]{0,2,1:T(8,128)(2,1)}, bf16[256,2,1024]{0,2,1:T(8,128)(2,1)}, u32[]{:S(2)}, u32[]{:S(2)}) %collective-permute-start) | collective-permute-done | bytes 1048608 | tf_op jit(solution)/shard_map/while/body/eval_jaxpr/ppermute | solution.py:19
  356.2 16.9 %collective-permute-done = bf16[256,2,1024]{0,2,1:T(8,128)(2,1)} collective-permute-done((bf16[256,2,1024]{0,2,1:T(8,128)(2,1)}, bf16[256,2,1024]{0,2,1:T(8,128)(2,1)}, u32[]{:S(2)}, u32[]{:S(2)}) %collective-permute-start) | collective-permute-done | bytes 1048608 | tf_op jit(solution)/shard_map/while/body/eval_jaxpr/ppermute | solution.py:19
  377.9 18.1 %collective-permute-done = bf16[256,2,1024]{0,2,1:T(8,128)(2,1)} collective-permute-done((bf16[256,2,1024]{0,2,1:T(8,128)(2,1)}, bf16[256,2,1024]{0,2,1:T(8,128)(2,1)}, u32[]{:S(2)}, u32[]{:S(2)}) %collective-permute-start) | collective-permute-done | bytes 1048608 | tf_op jit(solution)/shard_map/while/body/eval_jaxpr/ppermute | solution.py:19
  400.8 18.1 %collective-permute-done = bf16[256,2,1024]{0,2,1:T(8,128)(2,1)} collective-permute-done((bf16[256,2,1024]{0,2,1:T(8,128)(2,1)}, bf16[256,2,1024]{0,2,1:T(8,128)(2,1)}, u32[]{:S(2)}, u32[]{:S(2)}) %collective-permute-start) | collective-permute-done | bytes 1048608 | tf_op jit(solution)/shard_map/while/body/eval_jaxpr/ppermute | solution.py:19
  423.7 18.1 %collective-permute-done = bf16[256,2,1024]{0,2,1:T(8,128)(2,1)} collective-permute-done((bf16[256,2,1024]{0,2,1:T(8,128)(2,1)}, bf16[256,2,1024]{0,2,1:T(8,128)(2,1)}, u32[]{:S(2)}, u32[]{:S(2)}) %collective-permute-start) | collective-permute-done | bytes 1048608 | tf_op jit(solution)/shard_map/while/body/eval_jaxpr/ppermute | solution.py:19
  446.5 18.1 %collective-permute-done = bf16[256,2,1024]{0,2,1:T(8,128)(2,1)} collective-permute-done((bf16[256,2,1024]{0,2,1:T(8,128)(2,1)}, bf16[256,2,1024]{0,2,1:T(8,128)(2,1)}, u32[]{:S(2)}, u32[]{:S(2)}) %collective-permute-start) | collective-permute-done | bytes 1048608 | tf_op jit(solution)/shard_map/while/body/eval_jaxpr/ppermute | solution.py:19
  469.4 18.1 %collective-permute-done = bf16[256,2,1024]{0,2,1:T(8,128)(2,1)} collective-permute-done((bf16[256,2,1024]{0,2,1:T(8,128)(2,1)}, bf16[256,2,1024]{0,2,1:T(8,128)(2,1)}, u32[]{:S(2)}, u32[]{:S(2)}) %collective-permute-start) | collective-permute-done | bytes 1048608 | tf_op jit(solution)/shard_map/while/body/eval_jaxpr/ppermute | solution.py:19
  492.3 18.1 %collective-permute-done = bf16[256,2,1024]{0,2,1:T(8,128)(2,1)} collective-permute-done((bf16[256,2,1024]{0,2,1:T(8,128)(2,1)}, bf16[256,2,1024]{0,2,1:T(8,128)(2,1)}, u32[]{:S(2)}, u32[]{:S(2)}) %collective-permute-start) | collective-permute-done | bytes 1048608 | tf_op jit(solution)/shard_map/while/body/eval_jaxpr/ppermute | solution.py:19
  515.1 18.1 %collective-permute-done = bf16[256,2,1024]{0,2,1:T(8,128)(2,1)} collective-permute-done((bf16[256,2,1024]{0,2,1:T(8,128)(2,1)}, bf16[256,2,1024]{0,2,1:T(8,128)(2,1)}, u32[]{:S(2)}, u32[]{:S(2)}) %collective-permute-start) | collective-permute-done | bytes 1048608 | tf_op jit(solution)/shard_map/while/body/eval_jaxpr/ppermute | solution.py:19
  538.0 18.1 %collective-permute-done = bf16[256,2,1024]{0,2,1:T(8,128)(2,1)} collective-permute-done((bf16[256,2,1024]{0,2,1:T(8,128)(2,1)}, bf16[256,2,1024]{0,2,1:T(8,128)(2,1)}, u32[]{:S(2)}, u32[]{:S(2)}) %collective-permute-start) | collective-permute-done | bytes 1048608 | tf_op jit(solution)/shard_map/while/body/eval_jaxpr/ppermute | solution.py:19
  560.9 18.1 %collective-permute-done = bf16[256,2,1024]{0,2,1:T(8,128)(2,1)} collective-permute-done((bf16[256,2,1024]{0,2,1:T(8,128)(2,1)}, bf16[256,2,1024]{0,2,1:T(8,128)(2,1)}, u32[]{:S(2)}, u32[]{:S(2)}) %collective-permute-start) | collective-permute-done | bytes 1048608 | tf_op jit(solution)/shard_map/while/body/eval_jaxpr/ppermute | solution.py:19
  583.7 18.1 %collective-permute-done = bf16[256,2,1024]{0,2,1:T(8,128)(2,1)} collective-permute-done((bf16[256,2,1024]{0,2,1:T(8,128)(2,1)}, bf16[256,2,1024]{0,2,1:T(8,128)(2,1)}, u32[]{:S(2)}, u32[]{:S(2)}) %collective-permute-start) | collective-permute-done | bytes 1048608 | tf_op jit(solution)/shard_map/while/body/eval_jaxpr/ppermute | solution.py:19
  607.7 63.2 %all-gather.12.cloned.1.call-done = bf16[256,5120]{1,0:T(8,128)(2,1)} async-done(((bf16[16,5120]{1,0:T(8,128)(2,1)}), bf16[256,5120]{1,0:T(8,128)(2,1)}) %all-gather.12.cloned.1.call-update) | async-done | bytes 2621456 | tf_op jit(solution)/shard_map/all_gather | solution.py:164
  670.9 5.2 fusion.53
  (290 shorter events, 149.7 us)
Async XLA Ops:
  6.5 66.6 %copy-start = (bf16[4,64,5120]{2,1,0:T(8,128)(2,1)S(1)}, bf16[4,64,5120]{2,1,0:T(8,128)(2,1)}, u32[]{:S(2)}) copy-start(bf16[4,64,5120]{2,1,0:T(8,128)(2,1)} %param.11) | copy-start | bytes 7864324
  6.5 70.8 %copy-start.11 = (bf16[320]{0:T(512)(128)(2,1)S(1)}, bf16[320]{0:T(512)(128)(2,1)}, u32[]{:S(2)}) copy-start(bf16[320]{0:T(512)(128)(2,1)} %param.15) | copy-start | bytes 1924
  6.5 70.8 %copy-start.13 = (s32[4,64]{1,0:T(4,128)S(1)}, s32[4,64]{1,0:T(4,128)}, u32[]{:S(2)}) copy-start(s32[4,64]{1,0:T(4,128)} %param.18) | copy-start | bytes 3076
  6.5 66.6 %all-gather.6.cloned.1.call-start = ((), (), s32[]{:S(2)}) async-start(), calls=%async_computation.1 | async-start | bytes 1392640 | tf_op jit(solution)/shard_map/all_gather | solution.py:116
  7.3 126.9 %all-gather.8.cloned.1.call-start = ((), (), s32[]{:S(2)}) async-start(), calls=%async_computation.2 | async-start | bytes 1114112 | tf_op jit(solution)/shard_map/all_gather | solution.py:125
  76.0 126.0 %all-gather.10.cloned.1.call-start = ((), (), s32[]{:S(2)}) async-start(), calls=%async_computation.3 | async-start | bytes 4177920 | tf_op jit(solution)/shard_map/all_gather | solution.py:111
  76.7 531.0 %all-gather.14.cloned.1.call-start = ((), (), s32[]{:S(2)}) async-start(), calls=%async_computation.5 | async-start | bytes 4177920 | tf_op jit(solution)/shard_map/all_gather | solution.py:168
  244.2 27.5 %all-to-all-start = ((bf16[16,16,320]{2,1,0:T(8,128)(2,1)}), bf16[16,16,320]{2,1,0:T(8,128)(2,1)}, u32[]{:S(2)}, u32[]{:S(2)}) async-start(bf16[16,16,320]{2,1,0:T(8,128)(2,1)} %constant_dynamic-update-slice_fusion), calls=%async_computation | async-start | bytes 393216 | tf_op jit(solution)/shard_map/all_to_all | solution.py:122
  260.1 410.8 %all-gather.12.cloned.1.call-start = ((), (), s32[]{:S(2)}) async-start(), calls=%async_computation.4 | async-start | bytes 2785280 | tf_op jit(solution)/shard_map/all_gather | solution.py:164
  277.9 13.3 %collective-permute-start = (bf16[256,2,1024]{0,2,1:T(8,128)(2,1)}, bf16[256,2,1024]{0,2,1:T(8,128)(2,1)}, u32[]{:S(2)}, u32[]{:S(2)}) collective-permute-start(bf16[256,2,1024]{0,2,1:T(8,128)(2,1)} %get-tuple-element.379), channel_id=1, source_target_pairs={{240,0},{0,16},{16,32},{32,48},{48,64},{64,80},{80,96},{96,112},{1... | collective-permute-start | bytes 3145736 | tf_op jit(solution)/shard_map/while/body/eval_jaxpr/ppermute | solution.py:19
  295.9 14.5 %collective-permute-start = (bf16[256,2,1024]{0,2,1:T(8,128)(2,1)}, bf16[256,2,1024]{0,2,1:T(8,128)(2,1)}, u32[]{:S(2)}, u32[]{:S(2)}) collective-permute-start(bf16[256,2,1024]{0,2,1:T(8,128)(2,1)} %get-tuple-element.379), channel_id=1, source_target_pairs={{240,0},{0,16},{16,32},{32,48},{48,64},{64,80},{80,96},{96,112},{1... | collective-permute-start | bytes 3145736 | tf_op jit(solution)/shard_map/while/body/eval_jaxpr/ppermute | solution.py:19
  315.1 14.5 %collective-permute-start = (bf16[256,2,1024]{0,2,1:T(8,128)(2,1)}, bf16[256,2,1024]{0,2,1:T(8,128)(2,1)}, u32[]{:S(2)}, u32[]{:S(2)}) collective-permute-start(bf16[256,2,1024]{0,2,1:T(8,128)(2,1)} %get-tuple-element.379), channel_id=1, source_target_pairs={{240,0},{0,16},{16,32},{32,48},{48,64},{64,80},{80,96},{96,112},{1... | collective-permute-start | bytes 3145736 | tf_op jit(solution)/shard_map/while/body/eval_jaxpr/ppermute | solution.py:19
  334.4 15.9 %collective-permute-start = (bf16[256,2,1024]{0,2,1:T(8,128)(2,1)}, bf16[256,2,1024]{0,2,1:T(8,128)(2,1)}, u32[]{:S(2)}, u32[]{:S(2)}) collective-permute-start(bf16[256,2,1024]{0,2,1:T(8,128)(2,1)} %get-tuple-element.379), channel_id=1, source_target_pairs={{240,0},{0,16},{16,32},{32,48},{48,64},{64,80},{80,96},{96,112},{1... | collective-permute-start | bytes 3145736 | tf_op jit(solution)/shard_map/while/body/eval_jaxpr/ppermute | solution.py:19
  355.0 18.2 %collective-permute-start = (bf16[256,2,1024]{0,2,1:T(8,128)(2,1)}, bf16[256,2,1024]{0,2,1:T(8,128)(2,1)}, u32[]{:S(2)}, u32[]{:S(2)}) collective-permute-start(bf16[256,2,1024]{0,2,1:T(8,128)(2,1)} %get-tuple-element.379), channel_id=1, source_target_pairs={{240,0},{0,16},{16,32},{32,48},{48,64},{64,80},{80,96},{96,112},{1... | collective-permute-start | bytes 3145736 | tf_op jit(solution)/shard_map/while/body/eval_jaxpr/ppermute | solution.py:19
  377.8 18.2 %collective-permute-start = (bf16[256,2,1024]{0,2,1:T(8,128)(2,1)}, bf16[256,2,1024]{0,2,1:T(8,128)(2,1)}, u32[]{:S(2)}, u32[]{:S(2)}) collective-permute-start(bf16[256,2,1024]{0,2,1:T(8,128)(2,1)} %get-tuple-element.379), channel_id=1, source_target_pairs={{240,0},{0,16},{16,32},{32,48},{48,64},{64,80},{80,96},{96,112},{1... | collective-permute-start | bytes 3145736 | tf_op jit(solution)/shard_map/while/body/eval_jaxpr/ppermute | solution.py:19
  400.7 18.2 %collective-permute-start = (bf16[256,2,1024]{0,2,1:T(8,128)(2,1)}, bf16[256,2,1024]{0,2,1:T(8,128)(2,1)}, u32[]{:S(2)}, u32[]{:S(2)}) collective-permute-start(bf16[256,2,1024]{0,2,1:T(8,128)(2,1)} %get-tuple-element.379), channel_id=1, source_target_pairs={{240,0},{0,16},{16,32},{32,48},{48,64},{64,80},{80,96},{96,112},{1... | collective-permute-start | bytes 3145736 | tf_op jit(solution)/shard_map/while/body/eval_jaxpr/ppermute | solution.py:19
  423.6 18.2 %collective-permute-start = (bf16[256,2,1024]{0,2,1:T(8,128)(2,1)}, bf16[256,2,1024]{0,2,1:T(8,128)(2,1)}, u32[]{:S(2)}, u32[]{:S(2)}) collective-permute-start(bf16[256,2,1024]{0,2,1:T(8,128)(2,1)} %get-tuple-element.379), channel_id=1, source_target_pairs={{240,0},{0,16},{16,32},{32,48},{48,64},{64,80},{80,96},{96,112},{1... | collective-permute-start | bytes 3145736 | tf_op jit(solution)/shard_map/while/body/eval_jaxpr/ppermute | solution.py:19
  446.4 18.2 %collective-permute-start = (bf16[256,2,1024]{0,2,1:T(8,128)(2,1)}, bf16[256,2,1024]{0,2,1:T(8,128)(2,1)}, u32[]{:S(2)}, u32[]{:S(2)}) collective-permute-start(bf16[256,2,1024]{0,2,1:T(8,128)(2,1)} %get-tuple-element.379), channel_id=1, source_target_pairs={{240,0},{0,16},{16,32},{32,48},{48,64},{64,80},{80,96},{96,112},{1... | collective-permute-start | bytes 3145736 | tf_op jit(solution)/shard_map/while/body/eval_jaxpr/ppermute | solution.py:19
  469.3 18.2 %collective-permute-start = (bf16[256,2,1024]{0,2,1:T(8,128)(2,1)}, bf16[256,2,1024]{0,2,1:T(8,128)(2,1)}, u32[]{:S(2)}, u32[]{:S(2)}) collective-permute-start(bf16[256,2,1024]{0,2,1:T(8,128)(2,1)} %get-tuple-element.379), channel_id=1, source_target_pairs={{240,0},{0,16},{16,32},{32,48},{48,64},{64,80},{80,96},{96,112},{1... | collective-permute-start | bytes 3145736 | tf_op jit(solution)/shard_map/while/body/eval_jaxpr/ppermute | solution.py:19
  492.2 18.2 %collective-permute-start = (bf16[256,2,1024]{0,2,1:T(8,128)(2,1)}, bf16[256,2,1024]{0,2,1:T(8,128)(2,1)}, u32[]{:S(2)}, u32[]{:S(2)}) collective-permute-start(bf16[256,2,1024]{0,2,1:T(8,128)(2,1)} %get-tuple-element.379), channel_id=1, source_target_pairs={{240,0},{0,16},{16,32},{32,48},{48,64},{64,80},{80,96},{96,112},{1... | collective-permute-start | bytes 3145736 | tf_op jit(solution)/shard_map/while/body/eval_jaxpr/ppermute | solution.py:19
  515.0 18.2 %collective-permute-start = (bf16[256,2,1024]{0,2,1:T(8,128)(2,1)}, bf16[256,2,1024]{0,2,1:T(8,128)(2,1)}, u32[]{:S(2)}, u32[]{:S(2)}) collective-permute-start(bf16[256,2,1024]{0,2,1:T(8,128)(2,1)} %get-tuple-element.379), channel_id=1, source_target_pairs={{240,0},{0,16},{16,32},{32,48},{48,64},{64,80},{80,96},{96,112},{1... | collective-permute-start | bytes 3145736 | tf_op jit(solution)/shard_map/while/body/eval_jaxpr/ppermute | solution.py:19
  537.9 18.2 %collective-permute-start = (bf16[256,2,1024]{0,2,1:T(8,128)(2,1)}, bf16[256,2,1024]{0,2,1:T(8,128)(2,1)}, u32[]{:S(2)}, u32[]{:S(2)}) collective-permute-start(bf16[256,2,1024]{0,2,1:T(8,128)(2,1)} %get-tuple-element.379), channel_id=1, source_target_pairs={{240,0},{0,16},{16,32},{32,48},{48,64},{64,80},{80,96},{96,112},{1... | collective-permute-start | bytes 3145736 | tf_op jit(solution)/shard_map/while/body/eval_jaxpr/ppermute | solution.py:19
  560.8 18.2 %collective-permute-start = (bf16[256,2,1024]{0,2,1:T(8,128)(2,1)}, bf16[256,2,1024]{0,2,1:T(8,128)(2,1)}, u32[]{:S(2)}, u32[]{:S(2)}) collective-permute-start(bf16[256,2,1024]{0,2,1:T(8,128)(2,1)} %get-tuple-element.379), channel_id=1, source_target_pairs={{240,0},{0,16},{16,32},{32,48},{48,64},{64,80},{80,96},{96,112},{1... | collective-permute-start | bytes 3145736 | tf_op jit(solution)/shard_map/while/body/eval_jaxpr/ppermute | solution.py:19
  583.6 18.2 %collective-permute-start = (bf16[256,2,1024]{0,2,1:T(8,128)(2,1)}, bf16[256,2,1024]{0,2,1:T(8,128)(2,1)}, u32[]{:S(2)}, u32[]{:S(2)}) collective-permute-start(bf16[256,2,1024]{0,2,1:T(8,128)(2,1)} %get-tuple-element.379), channel_id=1, source_target_pairs={{240,0},{0,16},{16,32},{32,48},{48,64},{64,80},{80,96},{96,112},{1... | collective-permute-start | bytes 3145736 | tf_op jit(solution)/shard_map/while/body/eval_jaxpr/ppermute | solution.py:19
  (11 other events, 110.3 us)
Sparse Core Ops, SparseCore 0:
  9.2 63.9 all-gather.5
  76.1 58.0 all-gather.7
  136.0 65.9 all-gather.9
  203.6 73.8 all-gather.13
  607.7 63.0 all-gather.11
